TPU v7x, 128 devices: a whole 4x4x4 slice. The times are simulated.
128 devices in a mesh: gx: 8 (over y, core), gy: 16 (over x, z).
Axes of the slice: x: 4, y: 4, z: 4, core: 2. Of those that a mesh axis runs over, the one named last changes fastest.
Arguments:
- ocean_state: float32 [2048, 4, 32, 128], P(('gx', 'gy')), may hold values from -3 to 3
- land_mask: int32 [2048, 32, 128], P(('gx', 'gy')), may hold values 0 or 1
- ocean_map: int32 [2048], P(('gx', 'gy')), may hold values from 0 to 2047, as said below
- ice_motion: float32 [2048, 5, 32, 128], P(('gx', 'gy')), may hold values from -3 to 3
- ice_mass: float32 [2048, 32, 128], P(('gx', 'gy')), may hold values from 0.5 to 2
- ice_strength: float32 [2048, 32, 128], P(('gx', 'gy')), may hold values from 0.5 to 2
- ice_mask: int32 [2048, 32, 128], P(('gx', 'gy')), may hold values 0 or 1
- ice_map: int32 [2048], P(('gx', 'gy')), may hold values from 0 to 2047, as said below
Outputs:
- ice_result: float32 [2048, 5, 32, 128], P(('gx', 'gy'))
- ocean_stress: float32 [2048, 2, 32, 128], P(('gx', 'gy'))
Inputs may be any that keep to these rules, and one draw needn't show every extreme that they name: ocean_map and ice_map each name every block once. The 16 slots of device (gx, gy) hold blocks of block rows gx * 1 to gx + 1 - 1 only, and for every c exactly 1 of them lie in block columns c * 16 to c * 16 + 15. `ice_map`: as for ocean_map, drawn independently.
All inputs are finite; a program needn't handle non-finite values. No bound on the sum of `land_mask` or of `ice_mask` on one device may be relied on, other than what follows from the above.
Results may differ from a plain program's by a relative error of at most 0.00019.
Values sent between devices are 32-bit elements; how exact they have to be, the bound alone decides.
A program may use at most 192 MiB of HBM per device.

v0:
```python
import functools

import jax
import jax.numpy as jnp
from jax import lax
from jax.experimental import pallas as pl
from jax.experimental.pallas import tpu as pltpu
from jax.sharding import PartitionSpec as P

BH = 32
BW = 128
NP = 16
NX = 8
ITERS = 8
DEEP = 16
HIGH = BH + 2 * DEEP
NBLK = NP + 1
EDGE = 8
ROWS = HIGH + 2 * EDGE
MESH = pl.DeviceIdType.MESH
F32 = jnp.float32

GROUPS = (
    (("u", "i"), ("v", "i"), ("p", "i")),
    (("s1", "i"), ("s2", "i"), ("s12", "i")),
    (("m", "i"), ("uo", "o"), ("vo", "o")),
    (("tx", "o"), ("ty", "o"), ("ac", "o")),
)
NG = len(GROUPS)
PER = 3
SIDE_SETS = (("u", "v", "p", "s1", "s2", "s12"), ("m", "uo", "vo", "tx", "ty", "ac"))
TILE_FIELDS = ("u", "v", "p", "s1", "s2", "s12", "m", "uo", "vo", "tx", "ty", "ac", "sa", "sc")


def shifted(col, k, sign):
    dx, dz = lax.div(k, 4), lax.rem(k, 4)
    x, z = lax.div(col, 4), lax.rem(col, 4)
    return lax.rem(x + sign * dx + 4, 4) * 4 + lax.rem(z + sign * dz + 4, 4)


def tile_col(block_id):
    return lax.rem(lax.div(block_id, NP), NP)


def x_difference(ref, off, j, lane):
    sl = pl.ds(EDGE + off, 8)
    here = ref[j, sl]
    up = pltpu.roll(jnp.where(lane == 0, ref[(j + 1) % NBLK, sl], here), BW - 1, 1)
    down = pltpu.roll(jnp.where(lane == BW - 1, ref[(j - 1) % NBLK, sl], here), 1, 1)
    return up - down


def y_difference(ref, off, j):
    return ref[j, pl.ds(EDGE + off + 1, 8)] - ref[j, pl.ds(EDGE + off - 1, 8)]


def stress_rows(t, off, j, lane):
    sl = pl.ds(EDGE + off, 8)
    east = x_difference(t["u"], off, j, lane)
    north = y_difference(t["v"], off, j)
    shear = y_difference(t["u"], off, j) + x_difference(t["v"], off, j, lane)
    diverg = east + north
    tension = east - north
    square = diverg * diverg + (tension * tension + shear * shear) * 0.25 + 0.16
    p = t["p"][j, sl]
    ratio = p * lax.rsqrt(square)
    s1 = 0.4 * t["s1"][j, sl] + (ratio * diverg - p)
    s2 = 0.4 * t["s2"][j, sl] + ratio * tension
    s12 = 0.4 * t["s12"][j, sl] + ratio * shear
    quarter = 0.25 * s2
    t["s1"][j, sl] = s1
    t["s2"][j, sl] = s2
    t["s12"][j, sl] = s12
    t["sa"][j, sl] = s1 + quarter
    t["sc"][j, sl] = s1 - quarter


def momentum_rows(t, off, j, lane):
    sl = pl.ds(EDGE + off, 8)
    force_x = x_difference(t["sa"], off, j, lane) * 0.25 + y_difference(t["s12"], off, j) * 0.0625
    force_y = x_difference(t["s12"], off, j, lane) * 0.0625 + y_difference(t["sc"], off, j) * 0.25
    u, v, m = t["u"][j, sl], t["v"][j, sl], t["m"][j, sl]
    uo, vo = t["uo"][j, sl], t["vo"][j, sl]
    diff_x, diff_y = uo - u, vo - v
    square = diff_x * diff_x + diff_y * diff_y + 0.01
    drag = square * lax.rsqrt(square)
    diag = m + drag
    rotate = 0.5 * m
    rhs_x = m * (u - t["tx"][j, sl]) + force_x + drag * uo
    rhs_y = m * (v - t["ty"][j, sl]) + force_y + drag * vo
    scale = t["ac"][j, sl] * pltpu.reciprocal(diag * diag + rotate * rotate, approx=True)
    t["u"][j, sl] = (diag * rhs_x + rotate * rhs_y) * scale
    t["v"][j, sl] = (diag * rhs_y - rotate * rhs_x) * scale


def body(
    omap, imap, ocean_h, land_h, motion_h, mass_h, strength_h, mask_h,
    ice_out, ocean_out,
    ocean, land, motion, mass, strength, mask,
    send, recv, top, bottom, ids_send, ids_recv, ids_top, ids_bottom, order_v, inverse_v,
    order, inverse, side_send, side_recv, back_ice, back_ocean, tile,
    in_sem, id_s, id_r, idf_s, idf_r, small_sem, data_s, data_r,
    top_s, top_r, bot_s, bot_r, side_s, side_r, back_s, back_r, own_sem,
):
    gx, gy = lax.axis_index("gx"), lax.axis_index("gy")
    t = dict(zip(TILE_FIELDS, tile))
    lane = lax.broadcasted_iota(jnp.int32, (8, BW), 1)
    row8 = lax.broadcasted_iota(jnp.int32, (8, BW), 0)

    barrier = pltpu.get_barrier_semaphore()

    def greet(k, _):
        pl.semaphore_signal(barrier, inc=1, device_id=(gx, shifted(gy, k, 1)), device_id_type=MESH)
        return 0

    lax.fori_loop(1, NP, greet, 0)
    for d in (1, NX - 1):
        pl.semaphore_signal(
            barrier, inc=1, device_id=(lax.rem(gx + d, NX), gy), device_id_type=MESH
        )
    loads = [
        pltpu.make_async_copy(motion_h, motion, in_sem.at[0]),
        pltpu.make_async_copy(strength_h, strength, in_sem.at[1]),
        pltpu.make_async_copy(mass_h, mass, in_sem.at[2]),
        pltpu.make_async_copy(mask_h, mask, in_sem.at[3]),
        pltpu.make_async_copy(ocean_h, ocean, in_sem.at[4]),
        pltpu.make_async_copy(land_h, land, in_sem.at[5]),
    ]
    for load in loads:
        load.start()

    tile_of = lax.broadcasted_iota(jnp.int32, (NP, NP), 0)
    slot_of = lax.broadcasted_iota(jnp.int32, (NP, NP), 1)
    places = []
    for row, blocks in ((0, imap), (1, omap)):
        block = jnp.broadcast_to(blocks[...], (NP, NP))
        same = tile_col(block) == tile_of
        slot = jnp.max(jnp.where(same, slot_of, 0), axis=1, keepdims=True)
        place_in = jnp.max(jnp.where(same, lax.rem(block, NP), 0), axis=1, keepdims=True)
        order_v[row] = jnp.broadcast_to(slot, (NP, BW))
        places.append(jnp.broadcast_to(place_in, (NP, BW)))
    order_copy = pltpu.make_async_copy(order_v, order, small_sem.at[0])
    order_copy.start()
    for c in range(NP):
        ids_send[c] = jnp.where(row8 == 0, places[0][c : c + 1], places[1][c : c + 1])
    ids_recv[0] = ids_send[gy]
    order_copy.wait()

    def packed(name, si, so):
        if name == "p":
            return strength[si] * 0.3
        if name == "m":
            return mass[si] * mask[si].astype(F32)
        if name == "ac":
            return (1 - land[so]).astype(F32)
        if name in ("u", "v", "s1"):
            return motion[si, ("u", "v", "s1").index(name)]
        if name == "s2":
            return motion[si, 3] * 4.0
        if name == "s12":
            return motion[si, 4] * 8.0
        return ocean[so, ("uo", "vo", "tx", "ty").index(name)]

    def pack(g):
        def one(k, _):
            c = shifted(gy, k, 1)
            si, so = order[0, c, 0], order[1, c, 0]
            for f, (name, _kind) in enumerate(GROUPS[g]):
                send[g, k, f] = packed(name, si, so)
            return 0

        lax.fori_loop(1, NP, one, 0)
        si, so = order[0, gy, 0], order[1, gy, 0]
        for f, (name, _kind) in enumerate(GROUPS[g]):
            recv[g][0, f] = packed(name, si, so)

    def data_copy(g, k):
        return pltpu.make_async_remote_copy(
            src_ref=send.at[g, k], dst_ref=recv[g].at[k],
            send_sem=data_s.at[g, k], recv_sem=data_r.at[g, k],
            device_id=(gx, shifted(gy, k, 1)), device_id_type=MESH,
        )

    def id_copy(k):
        return pltpu.make_async_remote_copy(
            src_ref=ids_send.at[shifted(gy, k, 1)], dst_ref=ids_recv.at[k],
            send_sem=id_s.at[k], recv_sem=id_r.at[k],
            device_id=(gx, shifted(gy, k, 1)), device_id_type=MESH,
        )

    def top_copy(g, k):
        return pltpu.make_async_remote_copy(
            src_ref=recv[g].at[k, :, pl.ds(DEEP, DEEP)], dst_ref=top[g].at[k],
            send_sem=top_s.at[g, k], recv_sem=top_r.at[g, k],
            device_id=(gx + 1, gy), device_id_type=MESH,
        )

    def bottom_copy(g, k):
        return pltpu.make_async_remote_copy(
            src_ref=recv[g].at[k, :, pl.ds(0, DEEP)], dst_ref=bottom[g].at[k],
            send_sem=bot_s.at[g, k], recv_sem=bot_r.at[g, k],
            device_id=(gx - 1, gy), device_id_type=MESH,
        )

    def id_forward(d):
        return pltpu.make_async_remote_copy(
            src_ref=ids_recv, dst_ref=(ids_top, ids_bottom)[d],
            send_sem=idf_s.at[d], recv_sem=idf_r.at[d],
            device_id=((gx + 1, gx - 1)[d], gy), device_id_type=MESH,
        )

    def each(lo, fn):
        def step(k, _):
            fn(k)
            return 0

        lax.fori_loop(lo, NP, step, 0)

    loads[0].wait()
    loads[1].wait()
    pack(0)
    pl.semaphore_wait(barrier, NP - 1 + 2)
    each(1, lambda k: id_copy(k).start())
    each(1, lambda k: data_copy(0, k).start())
    pack(1)
    each(1, lambda k: data_copy(1, k).start())
    for load in loads[2:5]:
        load.wait()
    pack(2)
    each(1, lambda k: data_copy(2, k).start())
    loads[5].wait()
    pack(3)
    each(1, lambda k: data_copy(3, k).start())

    @pl.when(gx == 0)
    def _():
        ids_top[...] = jnp.zeros(ids_top.shape, jnp.int32)

        def clear(k):
            for g in range(NG):
                top[g][k] = jnp.zeros((PER, DEEP, BW), F32)

        each(0, clear)

    @pl.when(gx == NX - 1)
    def _():
        ids_bottom[...] = jnp.zeros(ids_bottom.shape, jnp.int32)

        def clear(k):
            for g in range(NG):
                bottom[g][k] = jnp.zeros((PER, DEEP, BW), F32)

        each(0, clear)

    for e in range(2):

        @pl.when(gy == (0, NP - 1)[e])
        def _():
            side_recv[:, e] = jnp.zeros((2, HIGH, BW), F32)

    for name in TILE_FIELDS:
        t[name][:, pl.ds(0, EDGE)] = jnp.zeros((NBLK, EDGE, BW), F32)
        t[name][:, pl.ds(ROWS - EDGE, EDGE)] = jnp.zeros((NBLK, EDGE, BW), F32)

    each(1, lambda k: id_copy(k).wait_recv())

    @pl.when(gx < NX - 1)
    def _():
        id_forward(0).start()

    @pl.when(gx > 0)
    def _():
        id_forward(1).start()

    def invert(which, source):
        found = jnp.zeros((8, BW), jnp.int32)
        for k in range(NP):
            found = jnp.maximum(found, jnp.where(source[k] == lane, k, 0))
        inverse_v[which] = found
        copy = pltpu.make_async_copy(inverse_v.at[which], inverse.at[which], small_sem.at[1 + which])
        copy.start()
        copy.wait()

    invert(0, ids_recv)
    place_of = jnp.zeros((8, BW), jnp.int32)
    for k in range(NP):
        place_of = jnp.where(lane == k, ids_recv[k], place_of)
    inverse_v[3] = place_of
    place_copy = pltpu.make_async_copy(inverse_v.at[3], inverse.at[3], small_sem.at[4])
    place_copy.start()
    place_copy.wait()

    @pl.when(gx > 0)
    def _():
        id_forward(0).wait_recv()

    invert(1, ids_top)

    @pl.when(gx < NX - 1)
    def _():
        id_forward(1).wait_recv()

    invert(2, ids_bottom)

    def forward(g, k):
        @pl.when(gx < NX - 1)
        def _():
            top_copy(g, k).start()

        @pl.when(gx > 0)
        def _():
            bottom_copy(g, k).start()

    def place(g, which, source, row, rows):
        def one(j):
            for f, (name, kind) in enumerate(GROUPS[g]):
                src = inverse[which, "io".index(kind), j]
                sl = pl.ds(EDGE + row, rows)
                value = source[src, f]
                if name == "ac":
                    value = jnp.where(t["m"][j, sl] > 0.0, value, 0.0)
                t[name][j, sl] = value

        each(0, one)

    def place_halo(g):
        @pl.when(gx > 0)
        def _():
            each(0, lambda k: top_copy(g, k).wait_recv())

        @pl.when(gx < NX - 1)
        def _():
            each(0, lambda k: bottom_copy(g, k).wait_recv())

        place(g, 1, top[g], 0, DEEP)
        place(g, 2, bottom[g], DEEP + BH, DEEP)

    def side_copy(n, e):
        return pltpu.make_async_remote_copy(
            src_ref=side_send.at[n, e], dst_ref=side_recv.at[n, e],
            send_sem=side_s.at[n, e], recv_sem=side_r.at[n, e],
            device_id=(gx, (gy + 1, gy - 1)[e]), device_id_type=MESH,
        )

    def send_sides(n):
        for a in range(HIGH // 8):
            right = jnp.zeros((8, BW), F32)
            left = jnp.zeros((8, BW), F32)
            for f, name in enumerate(SIDE_SETS[n]):
                here = (lane >= DEEP * f) & (lane < DEEP * (f + 1))
                r = t[name][NP - 1, pl.ds(EDGE + 8 * a, 8)]
                q = t[name][0, pl.ds(EDGE + 8 * a, 8)]
                right = jnp.where(here, pltpu.roll(r, (DEEP * f + DEEP) % BW, 1), right)
                left = jnp.where(here, pltpu.roll(q, DEEP * f, 1) if f else q, left)
            side_send[n, 0, pl.ds(8 * a, 8)] = right
            side_send[n, 1, pl.ds(8 * a, 8)] = left

        @pl.when(gy < NP - 1)
        def _():
            side_copy(n, 0).start()

        @pl.when(gy > 0)
        def _():
            side_copy(n, 1).start()

    def take_sides(n):
        @pl.when(gy > 0)
        def _():
            side_copy(n, 0).wait_recv()

        @pl.when(gy < NP - 1)
        def _():
            side_copy(n, 1).wait_recv()

        for a in range(HIGH // 8):
            left = side_recv[n, 0, pl.ds(8 * a, 8)]
            right = side_recv[n, 1, pl.ds(8 * a, 8)]
            for f, name in enumerate(SIDE_SETS[n]):
                r = pltpu.roll(right, BW - DEEP * f, 1) if f else right
                q = pltpu.roll(left, BW - DEEP - DEEP * f, 1)
                value = jnp.where(lane < DEEP, r, jnp.where(lane >= BW - DEEP, q, 0.0))
                t[name][NP, pl.ds(EDGE + 8 * a, 8)] = value

    def arrive(g):
        def one(k):
            data_copy(g, k).wait_recv()
            forward(g, k)

        forward(g, 0)
        each(1, one)
        place(g, 0, recv[g], DEEP, BH)

    arrive(0)
    arrive(1)
    place_halo(0)
    arrive(2)
    place_halo(1)
    send_sides(0)
    arrive(3)
    place_halo(2)
    place_halo(3)
    send_sides(1)
    take_sides(0)
    take_sides(1)

    def subcycle(n, _):
        skip_s, skip_m = lax.div(n, 4), lax.div(n + 1, 4)

        def stress_step(i, _):
            for a in range(2):
                off = (skip_s + 2 * i + a) * 8
                for j in range(NBLK):
                    stress_rows(t, off, j, lane)
            return 0

        lax.fori_loop(0, 4 - skip_s, stress_step, 0)

        def momentum_step(i, _):
            for a in range(2):
                off = (skip_m + 2 * i + a) * 8
                for j in range(NBLK):
                    momentum_rows(t, off, j, lane)
            return 0

        lax.fori_loop(0, 4 - skip_m, momentum_step, 0)
        return 0

    lax.fori_loop(0, ITERS, subcycle, 0)

    def back_copy(part, k):
        src, dst = (
            (back_ice.at[k, pl.ds(2, 3)], ice_out.at[k, pl.ds(2, 3)]),
            (back_ice.at[k, pl.ds(0, 2)], ice_out.at[k, pl.ds(0, 2)]),
            (back_ocean.at[k], ocean_out.at[k]),
        )[part]
        return pltpu.make_async_remote_copy(
            src_ref=src, dst_ref=dst, send_sem=back_s.at[part, k], recv_sem=back_r.at[part, k],
            device_id=(gx, shifted(gy, k, -1)), device_id_type=MESH,
        )

    def mine(name, at):
        return t[name][at, pl.ds(EDGE + DEEP, BH)]

    def pack_stress(k):
        at = inverse[3, 0, k]
        back_ice[k, 2] = mine("s1", at)
        back_ice[k, 3] = mine("s2", at) * 0.25
        back_ice[k, 4] = mine("s12", at) * 0.125

    def pack_velocity(k):
        at = inverse[3, 0, k]
        back_ice[k, 0] = mine("u", at)
        back_ice[k, 1] = mine("v", at)

    def pack_ocean(k):
        at = inverse[3, 1, k]
        diff_x = mine("u", at) - mine("uo", at)
        diff_y = mine("v", at) - mine("vo", at)
        square = diff_x * diff_x + diff_y * diff_y + 0.01
        drag = mine("ac", at) * (square * lax.rsqrt(square))
        back_ocean[k, 0] = drag * diff_x
        back_ocean[k, 1] = drag * diff_y

    def give_back(part, fill):
        def one(k):
            fill(k)
            back_copy(part, k).start()

        each(1, one)
        fill(0)

    give_back(0, pack_stress)
    give_back(1, pack_velocity)
    give_back(2, pack_ocean)
    own_ice = pltpu.make_async_copy(back_ice.at[0], ice_out.at[0], own_sem.at[0])
    own_ocean = pltpu.make_async_copy(back_ocean.at[0], ocean_out.at[0], own_sem.at[1])
    own_ice.start()
    own_ocean.start()

    def drain(k):
        id_copy(k).wait_send()
        for g in range(NG):
            data_copy(g, k).wait_send()

    each(1, drain)

    @pl.when(gx < NX - 1)
    def _():
        id_forward(0).wait_send()

        def one(k):
            for g in range(NG):
                top_copy(g, k).wait_send()

        each(0, one)

    @pl.when(gx > 0)
    def _():
        id_forward(1).wait_send()

        def one(k):
            for g in range(NG):
                bottom_copy(g, k).wait_send()

        each(0, one)

    @pl.when(gy < NP - 1)
    def _():
        for n in range(2):
            side_copy(n, 0).wait_send()

    @pl.when(gy > 0)
    def _():
        for n in range(2):
            side_copy(n, 1).wait_send()

    own_ice.wait()
    own_ocean.wait()

    def finish(k):
        for part in range(3):
            back_copy(part, k).wait_recv()

    each(1, finish)

    def finish_send(k):
        for part in range(3):
            back_copy(part, k).wait_send()

    each(1, finish_send)


def to_slots(omap, imap, ice_in, ocean_in, ice_out, ocean_out, ice_sem, ocean_sem):
    gy = lax.axis_index("gy")
    x, z = lax.div(gy, 4), lax.rem(gy, 4)

    def copies(s):
        found = []
        for blocks in (imap, omap):
            c = tile_col(blocks[s])
            cx, cz = lax.div(c, 4), lax.rem(c, 4)
            found.append(lax.rem(cx - x + 4, 4) * 4 + lax.rem(cz - z + 4, 4))
        return (
            pltpu.make_async_copy(ice_in.at[found[0]], ice_out.at[s], ice_sem.at[s]),
            pltpu.make_async_copy(ocean_in.at[found[1]], ocean_out.at[s], ocean_sem.at[s]),
        )

    started = [copies(s) for s in range(NP)]
    for pair in started:
        for copy in pair:
            copy.start()
    for pair in started:
        for copy in pair:
            copy.wait()


def shards(ocean_state, land_mask, ocean_map, ice_motion, ice_mass, ice_strength, ice_mask, ice_map):
    dma = pltpu.SemaphoreType.DMA
    vmem = pltpu.VMEM
    hbm = pl.BlockSpec(memory_space=pl.ANY)
    smem = pl.BlockSpec(memory_space=pltpu.SMEM)
    back = (
        jax.ShapeDtypeStruct((NP, 5, BH, BW), F32),
        jax.ShapeDtypeStruct((NP, 2, BH, BW), F32),
    )
    ids = vmem((NP, 8, BW), jnp.int32)
    ice_back, ocean_back = pl.pallas_call(
        body,
        out_shape=back,
        in_specs=[pl.BlockSpec(memory_space=pltpu.VMEM)] * 2 + [hbm] * 6,
        out_specs=(hbm, hbm),
        scratch_shapes=[
            vmem((NP, 4, BH, BW), F32),
            vmem((NP, BH, BW), jnp.int32),
            vmem((NP, 5, BH, BW), F32),
            vmem((NP, BH, BW), F32),
            vmem((NP, BH, BW), F32),
            vmem((NP, BH, BW), jnp.int32),
            vmem((NG, NP, PER, BH, BW), F32),
            [vmem((NP, PER, BH, BW), F32) for _ in GROUPS],
            [vmem((NP, PER, DEEP, BW), F32) for _ in GROUPS],
            [vmem((NP, PER, DEEP, BW), F32) for _ in GROUPS],
            ids, ids, ids, ids,
            vmem((2, NP, BW), jnp.int32),
            vmem((4, 8, BW), jnp.int32),
            pltpu.SMEM((2, NP, BW), jnp.int32),
            pltpu.SMEM((4, 8, BW), jnp.int32),
            vmem((2, 2, HIGH, BW), F32),
            vmem((2, 2, HIGH, BW), F32),
            vmem((NP, 5, BH, BW), F32),
            vmem((NP, 2, BH, BW), F32),
            [vmem((NBLK, ROWS, BW), F32) for _ in TILE_FIELDS],
            dma((6,)), dma((NP,)), dma((NP,)), dma((2,)), dma((2,)), dma((5,)),
            dma((NG, NP)), dma((NG, NP)),
            dma((NG, NP)), dma((NG, NP)), dma((NG, NP)), dma((NG, NP)),
            dma((2, 2)), dma((2, 2)), dma((3, NP)), dma((3, NP)), dma((2,)),
        ],
        compiler_params=pltpu.CompilerParams(
            collective_id=0, has_side_effects=True, vmem_limit_bytes=48 << 20
        ),
        cost_estimate=pl.CostEstimate(flops=100_000_000, bytes_accessed=6 << 20, transcendentals=0),
        name="ice_subcycles",
    )(ocean_map[None], ice_map[None], ocean_state, land_mask, ice_motion, ice_mass, ice_strength, ice_mask)
    return pl.pallas_call(
        to_slots,
        out_shape=back,
        in_specs=[smem, smem, hbm, hbm],
        out_specs=(hbm, hbm),
        scratch_shapes=[dma((NP,)), dma((NP,))],
        name="to_slots",
    )(ocean_map, ice_map, ice_back, ocean_back)


def solution(mesh):
    blocks = P(("gx", "gy"), None, None, None)
    layer = P(("gx", "gy"), None, None)
    slots = P(("gx", "gy"))
    return jax.shard_map(
        shards, mesh=mesh,
        in_specs=(blocks, layer, slots, blocks, layer, layer, layer, slots),
        out_specs=(blocks, blocks), check_vma=False,
    )
```

profile of v0, /device:TPU:16, one launch (start us, length us, event | category | flops | bytes accessed | tf_op | source)
XLA Modules:
  0.0 160.0 jit_solution(14747259277038285715)
XLA Ops:
  0.6 0.0 copy-start
  0.6 1.3 copy-done
  1.9 0.0 copy-start.2
  2.0 1.2 copy-done.2
  3.2 0.0 copy-start.4
  3.2 0.9 copy-done.4
  4.1 0.0 copy-start.5
  4.1 0.9 copy-done.5
  5.1 0.0 copy-start.6
  5.1 0.9 copy-done.6
  6.0 0.0 copy-start.7
  6.0 0.9 copy-done.7
  7.0 0.0 copy-start.8
  7.0 0.7 copy-done.8
  7.6 0.0 copy-start.9
  7.6 0.7 copy-done.9
  8.3 92.1 %ice_subcycles.1 = (f32[16,5,32,128]{3,2,1,0:T(8,128)S(1)}, f32[16,2,32,128]{3,2,1,0:T(8,128)S(1)}) custom-call(s32[1,16]{1,0:T(1,128)S(1)} %bitcast.2, s32[1,16]{1,0:T(1,128)S(1)} %bitcast.3, f32[16,4,32,128]{3,2,1,0:T(8,128)S(1)} %copy-done.2, s32[16,32,128]{2,1,0:T(8,128)S(1)} %copy-done.4, f32[16,5,32,128]{3,2,1,0:T(8,128)S(1)} %copy-done, ...), custom_call_target="tpu_custom_call" | custom-call | flops 100000000 | bytes 6291456 | tf_op jit(solution)/shard_map/ice_subcycles/pallas_call | solution.py:567
  100.4 0.0 copy-start.1
  100.4 1.1 copy-done.1
  101.5 0.0 copy-start.3
  101.5 0.8 copy-done.3
  102.4 57.7 %to_slots.1 = (f32[16,5,32,128]{3,2,1,0:T(8,128)}, f32[16,2,32,128]{3,2,1,0:T(8,128)}) custom-call(s32[16]{0:T(128)} %omap.1, s32[16]{0:T(128)} %imap.1, f32[16,5,32,128]{3,2,1,0:T(8,128)} %copy-done.1, f32[16,2,32,128]{3,2,1,0:T(8,128)} %copy-done.3), custom_call_target="tpu_custom_call" | custom-call | tf_op jit(solution)/shard_map/to_slots/pallas_call | solution.py:604
Async XLA Ops:
  0.6 1.3 copy-start
  1.9 1.2 copy-start.2
  3.2 0.9 copy-start.4
  4.1 0.9 copy-start.5
  5.1 0.9 copy-start.6
  6.0 0.9 copy-start.7
  7.0 0.7 copy-start.8
  7.6 0.7 copy-start.9
  100.4 1.1 copy-start.1
  101.5 0.8 copy-start.3
where the time goes:
time: 163 us; the launch traced here: 160 us
  Pallas kernels  150 us (92%)
  local copies, waits for them, and re-layouts  9.55 us (6%)
    pallas_call x1, Pallas kernels, shards(): pl.pallas_call(body, out_shape=back, in_specs=[pl.BlockSpec(memory_space=...  92.1 us
    pallas_call x1, Pallas kernels, shards(): pl.pallas_call(to_slots, out_shape=back, in_specs=[smem, smem, hbm, hbm],...  57.7 us
    unnamed x20, local copies, waits for them, and re-layouts  9.55 us

commit v1 on v0

--- a/solution.py
+++ b/solution.py
@@ -94,9 +94,9 @@
 
 
 def body(
-    omap, imap, ocean_h, land_h, motion_h, mass_h, strength_h, mask_h,
+    omap_h, imap_h, ocean_h, land_h, motion_h, mass_h, strength_h, mask_h,
     ice_out, ocean_out,
-    ocean, land, motion, mass, strength, mask,
+    omap, imap, ocean, land, motion, mass, strength, mask,
     send, recv, top, bottom, ids_send, ids_recv, ids_top, ids_bottom, order_v, inverse_v,
     order, inverse, side_send, side_recv, back_ice, back_ocean, tile,
     in_sem, id_s, id_r, idf_s, idf_r, small_sem, data_s, data_r,
@@ -118,6 +118,10 @@
         pl.semaphore_signal(
             barrier, inc=1, device_id=(lax.rem(gx + d, NX), gy), device_id_type=MESH
         )
+    map_loads = [
+        pltpu.make_async_copy(imap_h, imap, in_sem.at[6]),
+        pltpu.make_async_copy(omap_h, omap, in_sem.at[7]),
+    ]
     loads = [
         pltpu.make_async_copy(motion_h, motion, in_sem.at[0]),
         pltpu.make_async_copy(strength_h, strength, in_sem.at[1]),
@@ -126,8 +130,10 @@
         pltpu.make_async_copy(ocean_h, ocean, in_sem.at[4]),
         pltpu.make_async_copy(land_h, land, in_sem.at[5]),
     ]
-    for load in loads:
+    for load in map_loads + loads:
         load.start()
+    for load in map_loads:
+        load.wait()
 
     tile_of = lax.broadcasted_iota(jnp.int32, (NP, NP), 0)
     slot_of = lax.broadcasted_iota(jnp.int32, (NP, NP), 1)
@@ -530,35 +536,27 @@
     each(1, finish_send)
 
 
-def to_slots(omap, imap, ice_in, ocean_in, ice_out, ocean_out, ice_sem, ocean_sem):
+def to_slots(omap, imap, ice, ocean, ice_out, ocean_out, sem):
     gy = lax.axis_index("gy")
     x, z = lax.div(gy, 4), lax.rem(gy, 4)
-
-    def copies(s):
-        found = []
-        for blocks in (imap, omap):
+    copies = []
+    for n, (blocks, held, out) in enumerate(((imap, ice, ice_out), (omap, ocean, ocean_out))):
+        for s in range(NP):
             c = tile_col(blocks[s])
             cx, cz = lax.div(c, 4), lax.rem(c, 4)
-            found.append(lax.rem(cx - x + 4, 4) * 4 + lax.rem(cz - z + 4, 4))
-        return (
-            pltpu.make_async_copy(ice_in.at[found[0]], ice_out.at[s], ice_sem.at[s]),
-            pltpu.make_async_copy(ocean_in.at[found[1]], ocean_out.at[s], ocean_sem.at[s]),
-        )
-
-    started = [copies(s) for s in range(NP)]
-    for pair in started:
-        for copy in pair:
-            copy.start()
-    for pair in started:
-        for copy in pair:
-            copy.wait()
+            k = lax.rem(cx - x + 4, 4) * 4 + lax.rem(cz - z + 4, 4)
+            copies.append(pltpu.make_async_copy(held.at[k], out.at[s], sem.at[n, s]))
+            copies[-1].start()
+    for copy in copies:
+        copy.wait()
 
 
 def shards(ocean_state, land_mask, ocean_map, ice_motion, ice_mass, ice_strength, ice_mask, ice_map):
     dma = pltpu.SemaphoreType.DMA
     vmem = pltpu.VMEM
-    hbm = pl.BlockSpec(memory_space=pl.ANY)
+    hbm = pl.BlockSpec(memory_space=pltpu.HBM)
     smem = pl.BlockSpec(memory_space=pltpu.SMEM)
+    held = pl.BlockSpec(memory_space=pltpu.VMEM)
     back = (
         jax.ShapeDtypeStruct((NP, 5, BH, BW), F32),
         jax.ShapeDtypeStruct((NP, 2, BH, BW), F32),
@@ -567,9 +565,11 @@
     ice_back, ocean_back = pl.pallas_call(
         body,
         out_shape=back,
-        in_specs=[pl.BlockSpec(memory_space=pltpu.VMEM)] * 2 + [hbm] * 6,
+        in_specs=[hbm] * 8,
         out_specs=(hbm, hbm),
         scratch_shapes=[
+            vmem((1, NP), jnp.int32),
+            vmem((1, NP), jnp.int32),
             vmem((NP, 4, BH, BW), F32),
             vmem((NP, BH, BW), jnp.int32),
             vmem((NP, 5, BH, BW), F32),
@@ -590,7 +590,7 @@
             vmem((NP, 5, BH, BW), F32),
             vmem((NP, 2, BH, BW), F32),
             [vmem((NBLK, ROWS, BW), F32) for _ in TILE_FIELDS],
-            dma((6,)), dma((NP,)), dma((NP,)), dma((2,)), dma((2,)), dma((5,)),
+            dma((8,)), dma((NP,)), dma((NP,)), dma((2,)), dma((2,)), dma((5,)),
             dma((NG, NP)), dma((NG, NP)),
             dma((NG, NP)), dma((NG, NP)), dma((NG, NP)), dma((NG, NP)),
             dma((2, 2)), dma((2, 2)), dma((3, NP)), dma((3, NP)), dma((2,)),
@@ -600,13 +600,22 @@
         ),
         cost_estimate=pl.CostEstimate(flops=100_000_000, bytes_accessed=6 << 20, transcendentals=0),
         name="ice_subcycles",
-    )(ocean_map[None], ice_map[None], ocean_state, land_mask, ice_motion, ice_mass, ice_strength, ice_mask)
+    )(*[
+        pltpu.with_memory_space_constraint(array, pltpu.HBM)
+        for array in (
+            ocean_map[None], ice_map[None], ocean_state, land_mask,
+            ice_motion, ice_mass, ice_strength, ice_mask,
+        )
+    ])
     return pl.pallas_call(
         to_slots,
         out_shape=back,
-        in_specs=[smem, smem, hbm, hbm],
+        in_specs=[smem, smem, held, held],
         out_specs=(hbm, hbm),
-        scratch_shapes=[dma((NP,)), dma((NP,))],
+        scratch_shapes=[
+            dma((2, NP)),
+        ],
+        compiler_params=pltpu.CompilerParams(vmem_limit_bytes=16 << 20),
         name="to_slots",
     )(ocean_map, ice_map, ice_back, ocean_back)
 

time: 163 us -> 97.8 us (0.60)
  the two profiles are of different devices: /device:TPU:16 before, /device:TPU:19 now
where the time goes in v1:
time: 97.8 us; the launch traced here: 97.7 us
  Pallas kernels  97 us (99%)
    pallas_call x1, Pallas kernels, shards(): pl.pallas_call(body, out_shape=back, in_specs=[hbm] * 8, out_specs=(hbm,...  95 us
    pallas_call x1, Pallas kernels, shards(): pl.pallas_call(to_slots, out_shape=back, in_specs=[smem, smem, held, held...  2.06 us

profile of v1, /device:TPU:19, one launch (start us, length us, event | category | flops | bytes accessed | tf_op | source)
XLA Modules:
  0.0 97.7 jit_solution(6443435966703744771)
XLA Ops:
  0.6 0.0 copy-start
  0.6 0.0 copy-start.1
  0.7 95.0 %ice_subcycles.1 = (f32[16,5,32,128]{3,2,1,0:T(8,128)S(1)}, f32[16,2,32,128]{3,2,1,0:T(8,128)S(1)}) custom-call(s32[1,16]{1,0:T(1,128)} %bitcast.2, s32[1,16]{1,0:T(1,128)} %bitcast.3, f32[16,4,32,128]{3,2,1,0:T(8,128)} %ocean_h.1, s32[16,32,128]{2,1,0:T(8,128)} %land_h.1, f32[16,5,32,128]{3,2,1,0:T(8,128)} %motion_h.1, f32[16,32,128]{2,1,0:T(8,128)} %mass_h.1, ...), custom_call_target="tpu_custom_call" | custom-call | flops 100000000 | bytes 6291456 | tf_op jit(solution)/shard_map/ice_subcycles/pallas_call | solution.py:565
  95.6 0.0 copy-done
  95.6 0.0 copy-done.1
  95.6 2.1 %to_slots.1 = (f32[16,5,32,128]{3,2,1,0:T(8,128)}, f32[16,2,32,128]{3,2,1,0:T(8,128)}) custom-call(s32[16]{0:T(128)S(1)} %copy-done, s32[16]{0:T(128)S(1)} %copy-done.1, f32[16,5,32,128]{3,2,1,0:T(8,128)S(1)} %get-tuple-element.4.ice, f32[16,2,32,128]{3,2,1,0:T(8,128)S(1)} %get-tuple-element.5.ocean), custom_call_target="tpu_custom_call" | custom-call | tf_op jit(solution)/shard_map/to_slots/pallas_call | solution.py:610
Async XLA Ops:
  0.6 95.0 %copy-start = (s32[16]{0:T(128)S(1)}, s32[16]{0:T(128)}, u32[]{:S(2)}) copy-start(s32[16]{0:T(128)} %omap.1) | copy-start | bytes 196
  0.6 95.0 %copy-start.1 = (s32[16]{0:T(128)S(1)}, s32[16]{0:T(128)}, u32[]{:S(2)}) copy-start(s32[16]{0:T(128)} %imap.1) | copy-start | bytes 196

commit v2 on v1

v2 whole, which is shorter than its diff:
```python
import functools

import jax
import jax.numpy as jnp
from jax import lax
from jax.experimental import pallas as pl
from jax.experimental.pallas import tpu as pltpu
from jax.sharding import PartitionSpec as P

BH = 32
BW = 128
NP = 16
NX = 8
ITERS = 8
DEEP = 16
HIGH = BH + 2 * DEEP
EDGE = 24
CHUNK = 8
NC = BH // CHUNK
ROWS = HIGH + 2 * EDGE
MESH = pl.DeviceIdType.MESH
F32 = jnp.float32

ICE = ("u", "v", "p", "s1", "s2", "s12", "m")
OCEAN = ("uo", "vo", "tx", "ty", "ac")
FIELDS = ICE + OCEAN
NF = len(FIELDS)
SIDE_SETS = (FIELDS[:6], FIELDS[6:])
TILE_FIELDS = FIELDS + ("sa", "sc")
RESULTS = 7
OWN_ROW = (16, 24, 32, 40)
HALO_ROW = (8, 0, 56, 48)
SIDE_ROW = (16, 8, 24, 0, 32, 40, 48, 56)
SIDE_OWN = (0, 2, 4, 5)
SIDE_HALO = (1, 3, 7, 6)
NS = len(SIDE_ROW)


def shifted(col, k, sign):
    dx, dz = lax.div(k, 4), lax.rem(k, 4)
    x, z = lax.div(col, 4), lax.rem(col, 4)
    return lax.rem(x + sign * dx + 4, 4) * 4 + lax.rem(z + sign * dz + 4, 4)


def tile_col(block_id):
    return lax.rem(lax.div(block_id, NP), NP)


def x_difference(ref, off, j, lane):
    sl = pl.ds(EDGE + off, 8)
    here = ref[j, sl]
    if not isinstance(j, int):
        return pltpu.roll(here, BW - 1, 1) - pltpu.roll(here, 1, 1)
    up = pltpu.roll(jnp.where(lane == 0, ref[(j + 1) % NP, sl], here), BW - 1, 1)
    down = pltpu.roll(jnp.where(lane == BW - 1, ref[(j - 1) % NP, sl], here), 1, 1)
    return up - down


def y_difference(ref, off, j):
    return ref[j, pl.ds(EDGE + off + 1, 8)] - ref[j, pl.ds(EDGE + off - 1, 8)]


def stress_rows(t, off, j, lane):
    sl = pl.ds(EDGE + off, 8)
    east = x_difference(t["u"], off, j, lane)
    north = y_difference(t["v"], off, j)
    shear = y_difference(t["u"], off, j) + x_difference(t["v"], off, j, lane)
    diverg = east + north
    tension = east - north
    square = diverg * diverg + (tension * tension + shear * shear) * 0.25 + 0.16
    p = t["p"][j, sl]
    ratio = p * lax.rsqrt(square)
    s1 = 0.4 * t["s1"][j, sl] + (ratio * diverg - p)
    s2 = 0.4 * t["s2"][j, sl] + ratio * tension
    s12 = 0.4 * t["s12"][j, sl] + ratio * shear
    quarter = 0.25 * s2
    t["s1"][j, sl] = s1
    t["s2"][j, sl] = s2
    t["s12"][j, sl] = s12
    t["sa"][j, sl] = s1 + quarter
    t["sc"][j, sl] = s1 - quarter


def momentum_rows(t, off, j, lane):
    sl = pl.ds(EDGE + off, 8)
    force_x = x_difference(t["sa"], off, j, lane) * 0.25 + y_difference(t["s12"], off, j) * 0.0625
    force_y = x_difference(t["s12"], off, j, lane) * 0.0625 + y_difference(t["sc"], off, j) * 0.25
    u, v, m = t["u"][j, sl], t["v"][j, sl], t["m"][j, sl]
    uo, vo = t["uo"][j, sl], t["vo"][j, sl]
    diff_x, diff_y = uo - u, vo - v
    square = diff_x * diff_x + diff_y * diff_y + 0.01
    drag = square * lax.rsqrt(square)
    diag = m + drag
    rotate = 0.5 * m
    rhs_x = m * (u - t["tx"][j, sl]) + force_x + drag * uo
    rhs_y = m * (v - t["ty"][j, sl]) + force_y + drag * vo
    scale = t["ac"][j, sl] * pltpu.reciprocal(diag * diag + rotate * rotate, approx=True)
    t["u"][j, sl] = (diag * rhs_x + rotate * rhs_y) * scale
    t["v"][j, sl] = (diag * rhs_y - rotate * rhs_x) * scale


def body(
    omap_h, imap_h, ocean_h, land_h, motion_h, mass_h, strength_h, mask_h,
    out,
    omap, imap, ocean, land, motion, mass, strength, mask,
    send, recv, halo, ids_send, ids_recv, ids_up, ids_low, order_v, inverse_v,
    order, inverse, side_send, side_recv, back, tile, strip,
    in_sem, map_sem, id_s, id_r, idf_s, idf_r, small_sem, data_s, data_r,
    halo_s, halo_r, side_s, side_r, back_s, back_r, own_sem,
):
    gx, gy = lax.axis_index("gx"), lax.axis_index("gy")
    odd = lax.rem(gx, 2)
    sign = 1 - 2 * odd
    up, low = gx - sign, gx + sign
    has_up = (gx > 0) & (gx < NX - 1)
    t = dict(zip(TILE_FIELDS, tile))
    edge = dict(zip(TILE_FIELDS, strip))
    lane = lax.broadcasted_iota(jnp.int32, (8, BW), 1)
    row8 = lax.broadcasted_iota(jnp.int32, (8, BW), 0)

    def actual(row):
        return odd * (HIGH - 8) + sign * row

    def chunk_at(i):
        return odd * (BH - CHUNK) + sign * (CHUNK * i)

    barrier = pltpu.get_barrier_semaphore()

    def greet(k, _):
        pl.semaphore_signal(barrier, inc=1, device_id=(gx, shifted(gy, k, 1)), device_id_type=MESH)
        return 0

    lax.fori_loop(1, NP, greet, 0)
    for d in (1, NX - 1):
        pl.semaphore_signal(
            barrier, inc=1, device_id=(lax.rem(gx + d, NX), gy), device_id_type=MESH
        )
    map_loads = [
        pltpu.make_async_copy(imap_h, imap, map_sem.at[0]),
        pltpu.make_async_copy(omap_h, omap, map_sem.at[1]),
    ]
    loads = []
    for i in range(NC):
        rows = pl.ds(chunk_at(i), CHUNK)
        loads.append([
            pltpu.make_async_copy(motion_h.at[:, :, rows], motion[i], in_sem.at[i, 0]),
            pltpu.make_async_copy(strength_h.at[:, rows], strength[i], in_sem.at[i, 1]),
            pltpu.make_async_copy(mass_h.at[:, rows], mass[i], in_sem.at[i, 2]),
            pltpu.make_async_copy(mask_h.at[:, rows], mask[i], in_sem.at[i, 3]),
            pltpu.make_async_copy(ocean_h.at[:, :, rows], ocean[i], in_sem.at[i, 4]),
            pltpu.make_async_copy(land_h.at[:, rows], land[i], in_sem.at[i, 5]),
        ])
    for load in map_loads + sum(loads, []):
        load.start()
    for load in map_loads:
        load.wait()

    tile_of = lax.broadcasted_iota(jnp.int32, (NP, NP), 0)
    slot_of = lax.broadcasted_iota(jnp.int32, (NP, NP), 1)
    places = []
    found = jnp.zeros((8, BW), jnp.int32)
    lane16 = lax.broadcasted_iota(jnp.int32, (NP, BW), 1)
    row16 = lax.broadcasted_iota(jnp.int32, (NP, BW), 0)
    for row, blocks in ((0, imap), (1, omap)):
        block = jnp.broadcast_to(blocks[...], (NP, NP))
        same = tile_col(block) == tile_of
        slot = jnp.max(jnp.where(same, slot_of, 0), axis=1, keepdims=True)
        place_in = jnp.max(jnp.where(same, lax.rem(block, NP), 0), axis=1, keepdims=True)
        slot = jnp.broadcast_to(slot, (NP, BW))
        slot = jnp.max(jnp.where(lane16 == row16, slot, 0), axis=0, keepdims=True)
        found = jnp.where(row8 == row, slot, found)
        places.append(jnp.broadcast_to(place_in, (NP, BW)))
    order_v[...] = found
    order_copy = pltpu.make_async_copy(order_v, order, small_sem.at[0])
    order_copy.start()
    for c in range(NP):
        ids_send[c] = jnp.where(row8 == 0, places[0][c : c + 1], places[1][c : c + 1])
    ids_recv[0] = ids_send[gy]
    order_copy.wait()

    def packed(i, name, si, so):
        if name == "p":
            return strength[i][si] * 0.3
        if name == "m":
            return mass[i][si] * mask[i][si].astype(F32)
        if name == "ac":
            return (1 - land[i][so]).astype(F32)
        if name in ("u", "v", "s1"):
            return motion[i][si, ("u", "v", "s1").index(name)]
        if name == "s2":
            return motion[i][si, 3] * 4.0
        if name == "s12":
            return motion[i][si, 4] * 8.0
        return ocean[i][so, ("uo", "vo", "tx", "ty").index(name)]

    def each(lo, fn, hi=NP, unroll=None):
        def step(k, _):
            fn(k)
            return 0

        lax.fori_loop(lo, hi, step, 0, unroll=unroll)

    def pack(i):
        def one(k):
            c = shifted(gy, k, 1)
            si, so = order[0, c], order[1, c]
            for f, name in enumerate(FIELDS):
                send[i, k, f] = packed(i, name, si, so)

        each(1, one, unroll=5)
        si, so = order[0, gy], order[1, gy]
        for f, name in enumerate(FIELDS):
            recv[i][0, f] = packed(i, name, si, so)

    def data_copy(i, k):
        return pltpu.make_async_remote_copy(
            src_ref=send.at[i, k], dst_ref=recv[i].at[k],
            send_sem=data_s.at[i, k], recv_sem=data_r.at[i, k],
            device_id=(gx, shifted(gy, k, 1)), device_id_type=MESH,
        )

    def id_copy(k):
        return pltpu.make_async_remote_copy(
            src_ref=ids_send.at[shifted(gy, k, 1)], dst_ref=ids_recv.at[k],
            send_sem=id_s.at[k], recv_sem=id_r.at[k],
            device_id=(gx, shifted(gy, k, 1)), device_id_type=MESH,
        )

    def halo_copy(i, k):
        return pltpu.make_async_remote_copy(
            src_ref=recv[i].at[k], dst_ref=halo[i].at[k],
            send_sem=halo_s.at[i, k], recv_sem=halo_r.at[i, k],
            device_id=(up if i < 2 else low, gy), device_id_type=MESH,
        )

    def id_forward(d):
        return pltpu.make_async_remote_copy(
            src_ref=ids_recv, dst_ref=(ids_up, ids_low)[d],
            send_sem=idf_s.at[d], recv_sem=idf_r.at[d],
            device_id=((up, low)[d], gy), device_id_type=MESH,
        )

    for i in range(NC):
        for load in loads[i]:
            load.wait()
        pack(i)
        if i == 0:
            pl.semaphore_wait(barrier, NP - 1 + 2)
            each(1, lambda k: id_copy(k).start())
        each(1, lambda k: data_copy(i, k).start())

    @pl.when(jnp.logical_not(has_up))
    def _():
        for name in FIELDS:
            t[name][:, pl.ds(EDGE + odd * (HIGH - DEEP), DEEP)] = jnp.zeros((NP, DEEP, BW), F32)

    for e in range(2):

        @pl.when(gy == (0, NP - 1)[e])
        def _():
            side_recv[:, e] = jnp.zeros((NS, 2, 8, BW), F32)

    each(1, lambda k: id_copy(k).wait_recv())

    @pl.when(has_up)
    def _():
        id_forward(0).start()

    id_forward(1).start()

    def invert(which, source):
        found = jnp.zeros((8, BW), jnp.int32)
        for k in range(NP):
            found = jnp.maximum(found, jnp.where(source[k] == lane, k, 0))
        inverse_v[which] = found
        copy = pltpu.make_async_copy(
            inverse_v.at[which], inverse.at[which], small_sem.at[1 + which]
        )
        copy.start()
        copy.wait()

    invert(0, ids_recv)
    place_of = jnp.zeros((8, BW), jnp.int32)
    for k in range(NP):
        place_of = jnp.where(lane == k, ids_recv[k], place_of)
    inverse_v[3] = place_of
    place_copy = pltpu.make_async_copy(inverse_v.at[3], inverse.at[3], small_sem.at[4])
    place_copy.start()
    place_copy.wait()

    @pl.when(has_up)
    def _():
        id_forward(0).wait_recv()
        invert(1, ids_up)

    id_forward(1).wait_recv()
    invert(2, ids_low)

    def forward(i, k):
        if i < 2:

            @pl.when(has_up)
            def _():
                halo_copy(i, k).start()

        else:
            halo_copy(i, k).start()

    def arrive(i, lo, hi):
        def one(k):
            data_copy(i, k).wait_recv()
            forward(i, k)

        each(lo, one, hi)

    def place(which, source, row):
        sl = pl.ds(EDGE + row, CHUNK)

        def one(j):
            si, so = inverse[which, 0, j], inverse[which, 1, j]
            for f, name in enumerate(FIELDS):
                value = source[si if name in ICE else so, f]
                if name == "ac":
                    value = jnp.where(source[si, FIELDS.index("m")] > 0.0, value, 0.0)
                t[name][j, sl] = value

        each(0, one, unroll=4)

    def place_halo(i):
        def take():
            each(0, lambda k: halo_copy(i, k).wait_recv())
            place(1 if i < 2 else 2, halo[i], actual(HALO_ROW[i]))

        if i < 2:
            pl.when(has_up)(take)
        else:
            take()

    def side_copy(m, e):
        return pltpu.make_async_remote_copy(
            src_ref=side_send.at[m, e], dst_ref=side_recv.at[m, e],
            send_sem=side_s.at[m, e], recv_sem=side_r.at[m, e],
            device_id=(gx, (gy + 1, gy - 1)[e]), device_id_type=MESH,
        )

    def send_sides(m):
        sl = pl.ds(EDGE + actual(SIDE_ROW[m]), CHUNK)
        for n, names in enumerate(SIDE_SETS):
            right = jnp.zeros((8, BW), F32)
            left = jnp.zeros((8, BW), F32)
            for f, name in enumerate(names):
                here = (lane >= DEEP * f) & (lane < DEEP * (f + 1))
                r = t[name][NP - 1, sl]
                q = t[name][0, sl]
                right = jnp.where(here, pltpu.roll(r, (DEEP * f + DEEP) % BW, 1), right)
                left = jnp.where(here, pltpu.roll(q, DEEP * f, 1) if f else q, left)
                first = jnp.where((lane >= 16) & (lane < 48), pltpu.roll(q, 16, 1), 0.0)
                last = pltpu.roll(r, BW - 32, 1)
                edge[name][0, sl] = jnp.where((lane >= 64) & (lane < 96), last, first)
            side_send[m, 0, n] = right
            side_send[m, 1, n] = left

        @pl.when(gy < NP - 1)
        def _():
            side_copy(m, 0).start()

        @pl.when(gy > 0)
        def _():
            side_copy(m, 1).start()

    def take_sides(m, row):
        @pl.when(gy > 0)
        def _():
            side_copy(m, 0).wait_recv()

        @pl.when(gy < NP - 1)
        def _():
            side_copy(m, 1).wait_recv()

        sl = pl.ds(EDGE + actual(row), CHUNK)
        for n, names in enumerate(SIDE_SETS):
            left = side_recv[m, 0, n]
            right = side_recv[m, 1, n]
            for f, name in enumerate(names):
                q = pltpu.roll(left, BW - DEEP * f, 1) if f else left
                r = pltpu.roll(right, 96 - DEEP * f, 1) if f < 6 else right
                value = jnp.where((lane >= 96) & (lane < 112), r, edge[name][0, sl])
                edge[name][0, sl] = jnp.where(lane < DEEP, q, value)

    def lowest(row, windows):
        return odd * (HIGH - 8) + sign * row - 8 * (windows - 1) * (1 - odd)

    def half_step(rows_of, row, windows=1, strip_row=None, strip_windows=1, strip_at=0):
        off = lowest(row, windows)
        for i in range(windows):
            for j in range(NP):
                rows_of(t, off + 8 * i, j, lane)
        if strip_row is not None:
            off = lowest(strip_row, strip_windows)
            for i in range(strip_windows):
                rows_of(edge, off + 8 * i, jnp.int32(strip_at), lane)

    def wave(end, beside, strip_end, strip_windows=1, strip_at=0):
        def one(n):
            h = 2 * n + 1
            half_step(stress_rows, end - h, 1, strip_end - h, strip_windows, strip_at)
            half_step(momentum_rows, end - h - 1, 1, strip_end - h - 1, strip_windows, strip_at)
            beside(n)

        each(0, one, ITERS)

    def first_waves(beside):
        def one(n):
            each(0, lambda i: half_step(stress_rows, 23 - 2 * n - 16 * i, 2), lax.div(45 - 4 * n, 16))
            each(0, lambda i: half_step(momentum_rows, 22 - 2 * n - 16 * i, 2), lax.div(43 - 4 * n, 16))
            beside(n)

        each(0, one, ITERS)

    def strip_wave(end, beside):
        def one(n):
            stress_rows(edge, actual(end - 2 * n - 1), jnp.int32(0), lane)
            momentum_rows(edge, actual(end - 2 * n - 2), jnp.int32(0), lane)
            beside(n)

        each(0, one, ITERS)

    def back_copy(i, k):
        return pltpu.make_async_remote_copy(
            src_ref=back.at[i, k], dst_ref=out.at[k, :, pl.ds(chunk_at(i), CHUNK)],
            send_sem=back_s.at[i, k], recv_sem=back_r.at[i, k],
            device_id=(gx, shifted(gy, k, -1)), device_id_type=MESH,
        )

    def own_copy(i):
        return pltpu.make_async_copy(
            back.at[i, 0], out.at[0, :, pl.ds(chunk_at(i), CHUNK)], own_sem.at[i]
        )

    def give_back(i):
        sl = pl.ds(EDGE + actual(16 + CHUNK * i), CHUNK)
        for name in ("u", "v", "s1", "s2", "s12"):
            edges = edge[name][0, sl]
            t[name][0, sl] = jnp.where(lane < DEEP, pltpu.roll(edges, BW - 16, 1), t[name][0, sl])
            t[name][NP - 1, sl] = jnp.where(
                lane >= BW - DEEP, pltpu.roll(edges, 32, 1), t[name][NP - 1, sl]
            )

        def fill(k):
            at = inverse[3, 0, k]
            back[i, k, 0] = t["u"][at, sl]
            back[i, k, 1] = t["v"][at, sl]
            back[i, k, 2] = t["s1"][at, sl]
            back[i, k, 3] = t["s2"][at, sl] * 0.25
            back[i, k, 4] = t["s12"][at, sl] * 0.125
            at = inverse[3, 1, k]
            diff_x = t["u"][at, sl] - t["uo"][at, sl]
            diff_y = t["v"][at, sl] - t["vo"][at, sl]
            square = diff_x * diff_x + diff_y * diff_y + 0.01
            drag = t["ac"][at, sl] * (square * lax.rsqrt(square))
            back[i, k, 5] = drag * diff_x
            back[i, k, 6] = drag * diff_y

        def one(k):
            fill(k)
            back_copy(i, k).start()

        each(1, one, unroll=5)
        fill(0)
        own_copy(i).start()

    def own(i):
        place(0, recv[i], actual(OWN_ROW[i]))
        send_sides(SIDE_OWN[i])

    def other(i):
        place_halo(i)
        send_sides(SIDE_HALO[i])

    for i in range(2):
        forward(i, 0)
        arrive(i, 1, NP)
        own(i)
        other(i)
    forward(2, 0)

    def beside_first(n):
        @pl.when(n >= 4)
        def _():
            arrive(2, jnp.maximum(4 * n - 16, 1), 4 * n - 12)

    first_waves(beside_first)
    own(2)
    forward(3, 0)
    for m in range(4):
        take_sides(m, SIDE_ROW[m])

    def beside_second(n):
        @pl.when(n > 0)
        def _():
            arrive(3, n, n + 1)

    wave(32, beside_second, 24, 4)
    other(2)
    take_sides(4, 32)
    strip_wave(32, lambda n: arrive(3, ITERS + n, ITERS + n + 1))
    own(3)
    give_back(0)

    def last_waves(i):
        @pl.when(i > 1)
        def _():
            take_sides(3 + i, 24 + 8 * i)

        wave(32 + 8 * i, lambda n: None, 24 + 8 * i, 1, jnp.where(i == 1, 1, 0))

        @pl.when(i == 1)
        def _():
            other(3)

        @pl.when(i > 1)
        def _():
            give_back(i - 1)

    each(1, last_waves, NC)
    take_sides(7, 56)
    strip_wave(56, lambda n: None)
    give_back(3)

    def drain(k):
        id_copy(k).wait_send()
        for i in range(NC):
            data_copy(i, k).wait_send()

    each(1, drain)

    @pl.when(has_up)
    def _():
        id_forward(0).wait_send()

        def one(k):
            for i in range(2):
                halo_copy(i, k).wait_send()

        each(0, one)

    id_forward(1).wait_send()

    def drain_low(k):
        for i in range(2, NC):
            halo_copy(i, k).wait_send()

    each(0, drain_low)
    for e in range(2):

        @pl.when((gy < NP - 1, gy > 0)[e])
        def _():
            for m in range(NS):
                side_copy(m, e).wait_send()

    for i in range(NC):
        own_copy(i).wait()
        each(1, lambda k: back_copy(i, k).wait_recv())
    for i in range(NC):
        each(1, lambda k: back_copy(i, k).wait_send())


def to_slots(omap, imap, held, ice_out, ocean_out, sem):
    gy = lax.axis_index("gy")
    x, z = lax.div(gy, 4), lax.rem(gy, 4)
    copies = []
    for n, (blocks, fields, out) in enumerate(
        ((imap, pl.ds(0, 5), ice_out), (omap, pl.ds(5, 2), ocean_out))
    ):
        for s in range(NP):
            c = tile_col(blocks[s])
            cx, cz = lax.div(c, 4), lax.rem(c, 4)
            k = lax.rem(cx - x + 4, 4) * 4 + lax.rem(cz - z + 4, 4)
            copies.append(pltpu.make_async_copy(held.at[k, fields], out.at[s], sem.at[n, s]))
            copies[-1].start()
    for copy in copies:
        copy.wait()


def shards(ocean_state, land_mask, ocean_map, ice_motion, ice_mass, ice_strength, ice_mask, ice_map):
    dma = pltpu.SemaphoreType.DMA
    vmem = pltpu.VMEM
    hbm = pl.BlockSpec(memory_space=pltpu.HBM)
    smem = pl.BlockSpec(memory_space=pltpu.SMEM)
    held = pl.BlockSpec(memory_space=pltpu.VMEM)
    integers = jnp.int32
    ids = vmem((NP, 8, BW), integers)

    def each_stage(shape, dtype):
        return [vmem(shape, dtype) for _ in range(NC)]

    held_back = pl.pallas_call(
        body,
        out_shape=jax.ShapeDtypeStruct((NP, RESULTS, BH, BW), F32),
        in_specs=[hbm] * 8,
        out_specs=hbm,
        scratch_shapes=[
            vmem((1, NP), integers),
            vmem((1, NP), integers),
            each_stage((NP, 4, CHUNK, BW), F32),
            each_stage((NP, CHUNK, BW), integers),
            each_stage((NP, 5, CHUNK, BW), F32),
            each_stage((NP, CHUNK, BW), F32),
            each_stage((NP, CHUNK, BW), F32),
            each_stage((NP, CHUNK, BW), integers),
            vmem((NC, NP, NF, CHUNK, BW), F32),
            each_stage((NP, NF, CHUNK, BW), F32),
            each_stage((NP, NF, CHUNK, BW), F32),
            ids, ids, ids, ids,
            vmem((8, BW), integers),
            vmem((4, 8, BW), integers),
            pltpu.SMEM((8, BW), integers),
            pltpu.SMEM((4, 8, BW), integers),
            vmem((NS, 2, 2, 8, BW), F32),
            vmem((NS, 2, 2, 8, BW), F32),
            vmem((NC, NP, RESULTS, CHUNK, BW), F32),
            [vmem((NP, ROWS, BW), F32) for _ in TILE_FIELDS],
            [vmem((2, ROWS, BW), F32) for _ in TILE_FIELDS],
            dma((NC, 6)), dma((2,)), dma((NP,)), dma((NP,)), dma((2,)), dma((2,)), dma((5,)),
            dma((NC, NP)), dma((NC, NP)), dma((NC, NP)), dma((NC, NP)),
            dma((NS, 2)), dma((NS, 2)), dma((NC, NP)), dma((NC, NP)), dma((NC,)),
        ],
        compiler_params=pltpu.CompilerParams(
            collective_id=0, has_side_effects=True, vmem_limit_bytes=48 << 20
        ),
        cost_estimate=pl.CostEstimate(flops=100_000_000, bytes_accessed=6 << 20, transcendentals=0),
        name="ice_subcycles",
    )(*[
        pltpu.with_memory_space_constraint(array, pltpu.HBM)
        for array in (
            ocean_map[None], ice_map[None], ocean_state, land_mask,
            ice_motion, ice_mass, ice_strength, ice_mask,
        )
    ])
    return pl.pallas_call(
        to_slots,
        out_shape=(
            jax.ShapeDtypeStruct((NP, 5, BH, BW), F32),
            jax.ShapeDtypeStruct((NP, 2, BH, BW), F32),
        ),
        in_specs=[smem, smem, held],
        out_specs=(hbm, hbm),
        scratch_shapes=[
            dma((2, NP)),
        ],
        compiler_params=pltpu.CompilerParams(vmem_limit_bytes=16 << 20),
        name="to_slots",
    )(ocean_map, ice_map, held_back)


def solution(mesh):
    blocks = P(("gx", "gy"), None, None, None)
    layer = P(("gx", "gy"), None, None)
    slots = P(("gx", "gy"))
    return jax.shard_map(
        shards, mesh=mesh,
        in_specs=(blocks, layer, slots, blocks, layer, layer, layer, slots),
        out_specs=(blocks, blocks), check_vma=False,
    )
```

time: 97.8 us -> 85.3 us (0.87)
  the two profiles are of different devices: /device:TPU:19 before, /device:TPU:16 now
where the time goes in v2:
time: 85.3 us; the launch traced here: 84.8 us
  Pallas kernels  84.1 us (99%)
    pallas_call x1, Pallas kernels, shards(): pl.pallas_call(body, out_shape=jax.ShapeDtypeStruct((NP, RESULTS, BH, BW)...  82.1 us
    pallas_call x1, Pallas kernels, shards(): pl.pallas_call(to_slots, out_shape=(jax.ShapeDtypeStruct((NP, 5, BH, BW),...  2.06 us

profile of v2, /device:TPU:16, one launch (start us, length us, event | category | flops | bytes accessed | tf_op | source)
XLA Modules:
  0.0 84.8 jit_solution(1795719053924499332)
XLA Ops:
  0.6 0.0 copy-start
  0.6 0.0 copy-start.1
  0.7 82.1 %ice_subcycles.1.held = f32[16,7,32,128]{3,2,1,0:T(8,128)S(1)} custom-call(s32[1,16]{1,0:T(1,128)} %bitcast.2, s32[1,16]{1,0:T(1,128)} %bitcast.3, f32[16,4,32,128]{3,2,1,0:T(8,128)} %ocean_h.1, s32[16,32,128]{2,1,0:T(8,128)} %land_h.1, f32[16,5,32,128]{3,2,1,0:T(8,128)} %motion_h.1, f32[16,32,128]{2,1,0:T(8,128)} %mass_h.1, f32[16,32,128]{2,1,0:T(8,128)} %strength_h.1, ...), custom_call_target="tpu_custom_call" | custom-call | flops 100000000 | bytes 6291456 | tf_op jit(solution)/shard_map/ice_subcycles/pallas_call | solution.py:597
  82.7 0.0 copy-done
  82.7 0.0 copy-done.1
  82.8 2.1 %to_slots.1 = (f32[16,5,32,128]{3,2,1,0:T(8,128)}, f32[16,2,32,128]{3,2,1,0:T(8,128)}) custom-call(s32[16]{0:T(128)S(1)} %copy-done, s32[16]{0:T(128)S(1)} %copy-done.1, f32[16,7,32,128]{3,2,1,0:T(8,128)S(1)} %ice_subcycles.1.held), custom_call_target="tpu_custom_call" | custom-call | tf_op jit(solution)/shard_map/to_slots/pallas_call | solution.py:640
Async XLA Ops:
  0.6 82.1 %copy-start = (s32[16]{0:T(128)S(1)}, s32[16]{0:T(128)}, u32[]{:S(2)}) copy-start(s32[16]{0:T(128)} %omap.1) | copy-start | bytes 196
  0.6 82.1 %copy-start.1 = (s32[16]{0:T(128)S(1)}, s32[16]{0:T(128)}, u32[]{:S(2)}) copy-start(s32[16]{0:T(128)} %imap.1) | copy-start | bytes 196

commit v3 on v2

--- a/solution.py
+++ b/solution.py
@@ -34,6 +34,7 @@
 SIDE_OWN = (0, 2, 4, 5)
 SIDE_HALO = (1, 3, 7, 6)
 NS = len(SIDE_ROW)
+FAR_FIRST = (10, 2, 8, 6, 14, 9, 11, 5, 15, 7, 13, 1, 4, 3, 12)
 
 
 def shifted(col, k, sign):
@@ -200,14 +201,19 @@
 
         lax.fori_loop(lo, hi, step, 0, unroll=unroll)
 
-    def pack(i):
+    def mirrored(k):
+        return k + odd * ((4 - k // 4) % 4 * 4 + (4 - k % 4) % 4 - k)
+
+    def pack_and_send(i):
         def one(k):
             c = shifted(gy, k, 1)
             si, so = order[0, c], order[1, c]
             for f, name in enumerate(FIELDS):
                 send[i, k, f] = packed(i, name, si, so)
-
-        each(1, one, unroll=5)
+            data_copy(i, k).start()
+
+        for k in FAR_FIRST:
+            one(mirrored(k))
         si, so = order[0, gy], order[1, gy]
         for f, name in enumerate(FIELDS):
             recv[i][0, f] = packed(i, name, si, so)
@@ -243,11 +249,10 @@
     for i in range(NC):
         for load in loads[i]:
             load.wait()
-        pack(i)
         if i == 0:
             pl.semaphore_wait(barrier, NP - 1 + 2)
             each(1, lambda k: id_copy(k).start())
-        each(1, lambda k: data_copy(i, k).start())
+        pack_and_send(i)
 
     @pl.when(jnp.logical_not(has_up))
     def _():
@@ -465,7 +470,8 @@
             fill(k)
             back_copy(i, k).start()
 
-        each(1, one, unroll=5)
+        for k in FAR_FIRST:
+            one(mirrored(k))
         fill(0)
         own_copy(i).start()
 
@@ -560,9 +566,8 @@
 
     for i in range(NC):
         own_copy(i).wait()
-        each(1, lambda k: back_copy(i, k).wait_recv())
-    for i in range(NC):
-        each(1, lambda k: back_copy(i, k).wait_send())
+        each(1, lambda k: back_copy(i, k).wait_send(), unroll=5)
+        each(1, lambda k: back_copy(i, k).wait_recv(), unroll=5)
 
 
 def to_slots(omap, imap, held, ice_out, ocean_out, sem):

time: 85.3 us -> 83.3 us (0.977)
  Pallas kernels: 84.1 us -> 82.4 us
    pallas_call x1, Pallas kernels: 82.1 us -> 80.4 us  [shards(): pl.pallas_call(body, out_shape=jax.ShapeDtypeStruct((NP, RESULTS, BH, BW)...]
where the time goes in v3:
time: 83.3 us; the launch traced here: 83.1 us
  Pallas kernels  82.4 us (99%)
    pallas_call x1, Pallas kernels, shards(): pl.pallas_call(body, out_shape=jax.ShapeDtypeStruct((NP, RESULTS, BH, BW)...  80.4 us
    pallas_call x1, Pallas kernels, shards(): pl.pallas_call(to_slots, out_shape=(jax.ShapeDtypeStruct((NP, 5, BH, BW),...  2.06 us

profile of v3, /device:TPU:16, one launch (start us, length us, event | category | flops | bytes accessed | tf_op | source)
XLA Modules:
  0.0 83.1 jit_solution(11753233825765686382)
XLA Ops:
  0.6 0.0 copy-start
  0.6 0.0 copy-start.1
  0.7 80.4 %ice_subcycles.1.held = f32[16,7,32,128]{3,2,1,0:T(8,128)S(1)} custom-call(s32[1,16]{1,0:T(1,128)} %bitcast.2, s32[1,16]{1,0:T(1,128)} %bitcast.3, f32[16,4,32,128]{3,2,1,0:T(8,128)} %ocean_h.1, s32[16,32,128]{2,1,0:T(8,128)} %land_h.1, f32[16,5,32,128]{3,2,1,0:T(8,128)} %motion_h.1, f32[16,32,128]{2,1,0:T(8,128)} %mass_h.1, f32[16,32,128]{2,1,0:T(8,128)} %strength_h.1, ...), custom_call_target="tpu_custom_call" | custom-call | flops 100000000 | bytes 6291456 | tf_op jit(solution)/shard_map/ice_subcycles/pallas_call | solution.py:602
  81.0 0.0 copy-done
  81.1 0.0 copy-done.1
  81.1 2.1 %to_slots.1 = (f32[16,5,32,128]{3,2,1,0:T(8,128)}, f32[16,2,32,128]{3,2,1,0:T(8,128)}) custom-call(s32[16]{0:T(128)S(1)} %copy-done, s32[16]{0:T(128)S(1)} %copy-done.1, f32[16,7,32,128]{3,2,1,0:T(8,128)S(1)} %ice_subcycles.1.held), custom_call_target="tpu_custom_call" | custom-call | tf_op jit(solution)/shard_map/to_slots/pallas_call | solution.py:645
Async XLA Ops:
  0.6 80.4 %copy-start = (s32[16]{0:T(128)S(1)}, s32[16]{0:T(128)}, u32[]{:S(2)}) copy-start(s32[16]{0:T(128)} %omap.1) | copy-start | bytes 196
  0.6 80.4 %copy-start.1 = (s32[16]{0:T(128)S(1)}, s32[16]{0:T(128)}, u32[]{:S(2)}) copy-start(s32[16]{0:T(128)} %imap.1) | copy-start | bytes 196

commit v4 on v3

--- a/solution.py
+++ b/solution.py
@@ -125,6 +125,13 @@
     def chunk_at(i):
         return odd * (BH - CHUNK) + sign * (CHUNK * i)
 
+    map_loads = [
+        pltpu.make_async_copy(imap_h, imap, map_sem.at[0]),
+        pltpu.make_async_copy(omap_h, omap, map_sem.at[1]),
+    ]
+    for load in map_loads:
+        load.start()
+
     barrier = pltpu.get_barrier_semaphore()
 
     def greet(k, _):
@@ -136,10 +143,6 @@
         pl.semaphore_signal(
             barrier, inc=1, device_id=(lax.rem(gx + d, NX), gy), device_id_type=MESH
         )
-    map_loads = [
-        pltpu.make_async_copy(imap_h, imap, map_sem.at[0]),
-        pltpu.make_async_copy(omap_h, omap, map_sem.at[1]),
-    ]
     loads = []
     for i in range(NC):
         rows = pl.ds(chunk_at(i), CHUNK)
@@ -151,7 +154,7 @@
             pltpu.make_async_copy(ocean_h.at[:, :, rows], ocean[i], in_sem.at[i, 4]),
             pltpu.make_async_copy(land_h.at[:, rows], land[i], in_sem.at[i, 5]),
         ])
-    for load in map_loads + sum(loads, []):
+    for load in loads[0]:
         load.start()
     for load in map_loads:
         load.wait()
@@ -253,6 +256,9 @@
             pl.semaphore_wait(barrier, NP - 1 + 2)
             each(1, lambda k: id_copy(k).start())
         pack_and_send(i)
+        if i == 0:
+            for load in sum(loads[1:], []):
+                load.start()
 
     @pl.when(jnp.logical_not(has_up))
     def _():

time: 83.3 us -> 83.8 us (level)
  no operation moved by 1% of the time
where the time goes in v4:
time: 83.8 us; the launch traced here: 83.6 us
  Pallas kernels  82.9 us (99%)
    pallas_call x1, Pallas kernels, shards(): pl.pallas_call(body, out_shape=jax.ShapeDtypeStruct((NP, RESULTS, BH, BW)...  80.9 us
    pallas_call x1, Pallas kernels, shards(): pl.pallas_call(to_slots, out_shape=(jax.ShapeDtypeStruct((NP, 5, BH, BW),...  2.06 us

profile of v4, /device:TPU:16, one launch (start us, length us, event | category | flops | bytes accessed | tf_op | source)
XLA Modules:
  0.0 83.6 jit_solution(16181957907775919163)
XLA Ops:
  0.6 0.0 copy-start
  0.6 0.0 copy-start.1
  0.7 80.9 %ice_subcycles.1.held = f32[16,7,32,128]{3,2,1,0:T(8,128)S(1)} custom-call(s32[1,16]{1,0:T(1,128)} %bitcast.2, s32[1,16]{1,0:T(1,128)} %bitcast.3, f32[16,4,32,128]{3,2,1,0:T(8,128)} %ocean_h.1, s32[16,32,128]{2,1,0:T(8,128)} %land_h.1, f32[16,5,32,128]{3,2,1,0:T(8,128)} %motion_h.1, f32[16,32,128]{2,1,0:T(8,128)} %mass_h.1, f32[16,32,128]{2,1,0:T(8,128)} %strength_h.1, ...), custom_call_target="tpu_custom_call" | custom-call | flops 100000000 | bytes 6291456 | tf_op jit(solution)/shard_map/ice_subcycles/pallas_call | solution.py:608
  81.5 0.0 copy-done
  81.5 0.0 copy-done.1
  81.6 2.1 %to_slots.1 = (f32[16,5,32,128]{3,2,1,0:T(8,128)}, f32[16,2,32,128]{3,2,1,0:T(8,128)}) custom-call(s32[16]{0:T(128)S(1)} %copy-done, s32[16]{0:T(128)S(1)} %copy-done.1, f32[16,7,32,128]{3,2,1,0:T(8,128)S(1)} %ice_subcycles.1.held), custom_call_target="tpu_custom_call" | custom-call | tf_op jit(solution)/shard_map/to_slots/pallas_call | solution.py:651
Async XLA Ops:
  0.6 80.9 %copy-start = (s32[16]{0:T(128)S(1)}, s32[16]{0:T(128)}, u32[]{:S(2)}) copy-start(s32[16]{0:T(128)} %omap.1) | copy-start | bytes 196
  0.6 80.9 %copy-start.1 = (s32[16]{0:T(128)S(1)}, s32[16]{0:T(128)}, u32[]{:S(2)}) copy-start(s32[16]{0:T(128)} %imap.1) | copy-start | bytes 196
